TPU v7x, 32 devices: a whole 2x2x4 slice. The times are simulated.
32 devices in a mesh: dp: 8 (over z, y), tensor: 4 (over x, core).
Axes of the slice: x: 2, y: 2, z: 4, core: 2. Of those that a mesh axis runs over, the one named last changes fastest.
Arguments:
- tokens: bfloat16 [8192, 768], P(('dp', 'tensor')), may hold values from -6 to 6
- lengths: int32 [8, 2], P('dp'), may hold values from 256 to 768, as said below
- w_qkv: bfloat16 [768, 3, 768], P('dp', None, 'tensor'), may hold values from -0.21875 to 0.21875
- w_attn_out: bfloat16 [768, 768], P('tensor', 'dp'), may hold values from -0.625 to 0.625
- w_in: bfloat16 [768, 2, 1152], P('dp', None, 'tensor'), may hold values from -0.21875 to 0.21875
- w_mlp_out: bfloat16 [1152, 768], P('tensor', 'dp'), may hold values from -0.1875 to 0.1875
- gain_attn: bfloat16 [768], P('dp'), may hold values from 0.5 to 1.5
- gain_mlp: bfloat16 [768], P('dp'), may hold values from 0.5 to 1.5
- cotangent: bfloat16 [8192, 768], P(('dp', 'tensor')), may hold values from -6 to 6
Outputs:
- output: bfloat16 [8192, 768], P(('dp', 'tensor'))
- grad_tokens: bfloat16 [8192, 768], P(('dp', 'tensor'))
- grad_qkv: float32 [768, 3, 768], P('dp', None, 'tensor')
- grad_attn_out: float32 [768, 768], P('tensor', 'dp')
- grad_in: float32 [768, 2, 1152], P('dp', None, 'tensor')
- grad_mlp_out: float32 [1152, 768], P('tensor', 'dp')
- grad_gain_attn: float32 [768], P('dp')
- grad_gain_mlp: float32 [768], P('dp')
Inputs may be any that keep to these rules, and one draw needn't show every extreme that they name: Each row gives the lengths of the two sequences packed in order at the start of one group's 1024 slots; their sum lies above 768 and at most 1024, and in every draw some group's two lengths are 256 and 768.
All inputs are finite; a program needn't handle non-finite values.
Results may differ from a plain program's by a relative error of at most 0.02.
Values may be sent and summed in bfloat16 or wider, within the bound.
A program may use at most 128 MiB of HBM per device.

v0:
```python
import functools

import jax
import jax.numpy as jnp
from jax import lax
from jax.experimental import pallas as pl
from jax.experimental.pallas import tpu as pltpu
from jax.sharding import PartitionSpec as P

HEAD_DIM = 64
WINDOW = 128
NORM_EPS = 1e-05
ROPE_BASE = 10000.0
MASKED = -1e30
MESH = pl.DeviceIdType.MESH
BF = jnp.bfloat16
F32 = jnp.float32
NT = (((1,), (1,)), ((), ()))
VMEM = pl.BlockSpec(memory_space=pltpu.VMEM)
ANY = pl.BlockSpec(memory_space=pl.ANY)


def normal_rows(values):
    centre = values - jnp.mean(values, axis=-1, keepdims=True)
    spread = jnp.mean(centre * centre, axis=-1, keepdims=True)
    inv = lax.rsqrt(spread + NORM_EPS)
    return centre * inv, inv


def normal_back(values, grad):
    xhat, inv = normal_rows(values)
    mean_g = jnp.mean(grad, axis=-1, keepdims=True)
    mean_gx = jnp.mean(grad * xhat, axis=-1, keepdims=True)
    return inv * (grad - mean_g - xhat * mean_gx)


def remote(src, dst, send, recv, dev):
    return pltpu.make_async_remote_copy(
        src_ref=src, dst_ref=dst, send_sem=send, recv_sem=recv, device_id=dev, device_id_type=MESH
    )


def tensor_place():
    dp, t = lax.axis_index("dp"), lax.axis_index("tensor")
    x, core = lax.div(t, 2), lax.rem(t, 2)
    return dp, t, x, core, x * 2 + 1 - core, (1 - x) * 2 + core


def dp_place(dp_size):
    dp, t = lax.axis_index("dp"), lax.axis_index("tensor")
    return dp, t, lax.div(dp, 2), lax.rem(dp, 2), dp_size // 2


def greet(devices):
    barrier = pltpu.get_barrier_semaphore()
    for dev in devices:
        pl.semaphore_signal(barrier, inc=1, device_id=dev, device_id_type=MESH)
    pl.semaphore_wait(barrier, len(devices))


def tensor_peers():
    dp, t, x, core, corep, xp = tensor_place()
    return [(dp, corep), (dp, xp)]


def tensor_others(size):
    dp, t = lax.axis_index("dp"), lax.axis_index("tensor")
    return [(dp, lax.rem(t + k, size)) for k in range(1, size)]


def dp_peers(dp_size):
    dp, t, hi, lo, high = dp_place(dp_size)
    return [(hi * 2 + 1 - lo, t)] + [(lax.rem(hi + k, high) * 2 + lo, t) for k in range(1, high)]


class Gather:
    def __init__(self, src, out, sems):
        dp, t, x, core, corep, xp = tensor_place()
        send, recv, here = sems
        self.own = pltpu.make_async_copy(src, out.at[t], here)
        self.over_x = remote(src, out.at[t], send.at[0], recv.at[0], (dp, xp))
        self.to_core = remote(src, out.at[t], send.at[1], recv.at[1], (dp, corep))
        self.relay = remote(out.at[xp], out.at[xp], send.at[2], recv.at[2], (dp, corep))

    def start(self):
        self.over_x.start()
        self.to_core.start()
        self.own.start()

    def forward(self):
        self.over_x.wait_recv()
        self.relay.start()

    def finish(self):
        self.to_core.wait_recv()
        self.relay.wait_recv()
        self.over_x.wait_send()
        self.to_core.wait_send()
        self.relay.wait_send()
        self.own.wait()


GATHER_SEMS = [pltpu.SemaphoreType.DMA((3,)), pltpu.SemaphoreType.DMA((3,)), pltpu.SemaphoreType.DMA]


class ScatterSum:
    def __init__(self, part, scratch):
        self.part = part
        self.sbuf, self.r1, self.pbuf, self.r2, send, recv = scratch
        dp, t, x, core, corep, xp = tensor_place()
        self.place = (t, x, core, corep, xp)
        pair = (dp, corep)
        self.far = remote(self.sbuf.at[0], self.r1.at[0], send.at[0], recv.at[0], pair)
        self.near = remote(self.sbuf.at[1], self.r1.at[1], send.at[1], recv.at[1], pair)
        self.over = remote(self.pbuf, self.r2, send.at[2], recv.at[2], (dp, xp))

    def begin(self):
        t, x, core, corep, xp = self.place
        self.sbuf[0] = self.part((1 - x) * 2 + 1 - core).astype(BF)
        self.far.start()
        mine = self.part(xp)
        self.far.wait_recv()
        self.pbuf[...] = (mine + self.r1[0].astype(F32)).astype(BF)
        self.over.start()
        self.sbuf[1] = self.part(corep).astype(BF)
        self.near.start()

    def finish(self):
        total = self.part(self.place[0])
        self.near.wait_recv()
        total = total + self.r1[1].astype(F32)
        self.over.wait_recv()
        total = total + self.r2[...].astype(F32)
        for copy in (self.far, self.near, self.over):
            copy.wait_send()
        return total


class DpGather:
    def __init__(self, dp_size, slab, full, sems):
        zsend, zrecv, ysend, yrecv, here = sems
        dp, t, hi, lo, high = dp_place(dp_size)
        ypeer = (hi * 2 + 1 - lo, t)
        self.mine = pltpu.make_async_copy(slab, full.at[dp], here)
        self.ycopies = [remote(slab, full.at[dp], ysend.at[0], yrecv.at[0], ypeer)]
        self.zcopies = []
        for k in range(1, high):
            peer = (lax.rem(hi + k, high) * 2 + lo, t)
            self.zcopies.append(remote(slab, full.at[dp], zsend.at[k], zrecv.at[k], peer))
            block = lax.rem(hi - k + high, high) * 2 + lo
            self.ycopies.append(
                remote(full.at[block], full.at[block], ysend.at[k], yrecv.at[k], ypeer)
            )

    def start(self):
        self.ycopies[0].start()
        for copy in self.zcopies:
            copy.start()
        self.mine.start()

    def forward(self):
        for zcopy, ycopy in zip(self.zcopies, self.ycopies[1:]):
            zcopy.wait_recv()
            ycopy.start()

    def finish(self):
        for copy in self.ycopies:
            copy.wait_recv()
        for copy in self.ycopies + self.zcopies:
            copy.wait_send()
        self.mine.wait()


class DpScatter:
    def __init__(self, dp_size, grads, scratch):
        self.grads = grads
        self.ry, self.zs, self.zr, ysend, yrecv, zsend, zrecv = scratch
        dp, t, hi, lo, high = dp_place(dp_size)
        ypeer = (hi * 2 + 1 - lo, t)
        self.high = high
        self.ycopies, self.zcopies, self.blocks = [], [], []
        for k in range(high):
            block_hi = lax.rem(hi + k, high)
            self.blocks.append(block_hi * 2 + lo)
            self.ycopies.append(
                remote(
                    grads.at[block_hi * 2 + 1 - lo], self.ry.at[k], ysend.at[k], yrecv.at[k], ypeer
                )
            )
            if k:
                peer = (block_hi * 2 + lo, t)
                self.zcopies.append(
                    remote(self.zs.at[k], self.zr.at[k], zsend.at[k], zrecv.at[k], peer)
                )

    def start(self):
        for copy in self.ycopies[1:] + self.ycopies[:1]:
            copy.start()

    def forward(self):
        for k in range(1, self.high):
            self.ycopies[k].wait_recv()
            pair_sum = self.grads[self.blocks[k]].astype(F32) + self.ry[k].astype(F32)
            self.zs[k] = pair_sum.astype(BF)
            self.zcopies[k - 1].start()

    def finish(self):
        self.ycopies[0].wait_recv()
        total = self.grads[self.blocks[0]].astype(F32) + self.ry[0].astype(F32)
        for k in range(1, self.high):
            self.zcopies[k - 1].wait_recv()
            total = total + self.zr[k].astype(F32)
        for copy in self.ycopies + self.zcopies:
            copy.wait_send()
        return total


def dp_gather_sems(half):
    return [pltpu.SemaphoreType.DMA((half,))] * 4 + [pltpu.SemaphoreType.DMA]


def dp_scatter_scratch(half, own, width):
    return [pltpu.VMEM((half, own, width), BF)] * 3 + [pltpu.SemaphoreType.DMA((half,))] * 4


def scatter_scratch(rows, width):
    return [
        pltpu.VMEM((2, rows, width), BF),
        pltpu.VMEM((2, rows, width), BF),
        pltpu.VMEM((rows, width), BF),
        pltpu.VMEM((rows, width), BF),
        pltpu.SemaphoreType.DMA((3,)),
        pltpu.SemaphoreType.DMA((3,)),
    ]


def params(ident):
    return pltpu.CompilerParams(
        collective_id=ident, has_side_effects=True, vmem_limit_bytes=48 * 1024 * 1024
    )


def block_product(lhs_ref, w, low, high, rows):
    def part(b):
        lhs = lhs_ref[pl.ds(pl.multiple_of(b * rows, rows), rows), :]
        return lax.dot_general(lhs, w[:, low:high], NT, preferred_element_type=F32)

    return part


def first_kernel(dp_size, tok, cot, slab, xfull, cfull, wfull, xhat, *scr):
    gx, gc = Gather(xhat, xfull, scr[0:3]), Gather(cot, cfull, scr[3:6])
    weights = DpGather(dp_size, slab, wfull, scr[6:11])
    greet(tensor_peers() + dp_peers(dp_size))
    weights.start()
    xhat[...] = normal_rows(tok[...].astype(F32))[0].astype(BF)
    gx.start()
    gc.start()
    weights.forward()
    gx.forward()
    gc.forward()
    gx.finish()
    gc.finish()
    weights.finish()


def hidden_kernel(dp_size, c_attn, c_one, att, w, tok, slab, hid, x2full, w2full, xhat, *scr):
    rows = tok.shape[0]
    greet(tensor_peers() + dp_peers(dp_size))
    weights = DpGather(dp_size, slab, w2full, scr[9:14])
    weights.start()
    branch = ScatterSum(block_product(att, w, c_attn, c_one, rows), scr[3:9])
    branch.begin()
    hidden = tok[...].astype(F32) + branch.finish()
    hid[...] = hidden
    xhat[...] = normal_rows(hidden)[0].astype(BF)
    gather = Gather(xhat, x2full, scr[0:3])
    gather.start()
    weights.forward()
    gather.forward()
    gather.finish()
    weights.finish()


def middle_kernel(dp_size, c_in, dmix, w2, hid, cot, grads, dhid, dbfull, gsum, dbr, *scr):
    rows = hid.shape[0]
    greet(tensor_peers() + dp_peers(dp_size))
    weight_sum = DpScatter(dp_size, grads, scr[9:16])
    weight_sum.start()
    normed = ScatterSum(block_product(dmix, w2, 0, c_in, rows), scr[3:9])
    normed.begin()
    weight_sum.forward()
    d_hidden = cot[...].astype(F32) + normal_back(hid[...], normed.finish())
    dhid[...] = d_hidden
    dbr[...] = d_hidden.astype(BF)
    gather = Gather(dbr, dbfull, scr[0:3])
    gather.start()
    gather.forward()
    gsum[...] = weight_sum.finish()
    gather.finish()


def last_kernel(
    dp_size, t_size, c_attn, c_in, dproj, w, tok, dhid, grads, gated, w2, hid, raw_one, raw_two,
    gsum_two, gtok, out, gsum, gains, gbuf, grecv, gsend_sem, grecv_sem, *scr,
):
    rows = tok.shape[0]
    others = tensor_others(t_size)
    greet(others + dp_peers(dp_size))
    weight_sum = DpScatter(dp_size, grads, scr[12:19])
    weight_sum.start()
    normed = ScatterSum(block_product(dproj, w, 0, c_attn, rows), scr[0:6])
    result = ScatterSum(block_product(gated, w2, c_in, w2.shape[1], rows), scr[6:12])
    normed.begin()
    weight_sum.forward()
    result.begin()
    gtok[...] = (dhid[...] + normal_back(tok[...].astype(F32), normed.finish())).astype(BF)
    total = weight_sum.finish()
    gsum[...] = total
    gain_one = jnp.sum(total[:, :c_attn] * raw_one[...], axis=1, keepdims=True)
    gain_two = jnp.sum(gsum_two[:, :c_in] * raw_two[...], axis=1, keepdims=True)
    lane = lax.broadcasted_iota(jnp.int32, gbuf.shape, 1)
    gbuf[...] = jnp.where(lane < 64, gain_one, gain_two)
    copies = [
        remote(gbuf, grecv.at[k], gsend_sem.at[k], grecv_sem.at[k], peer)
        for k, peer in enumerate(others)
    ]
    for copy in copies:
        copy.start()
    out[...] = (hid[...] + result.finish()).astype(BF)
    gain_total = gbuf[...]
    for k, copy in enumerate(copies):
        copy.wait_recv()
        gain_total = gain_total + grecv[k]
    gains[...] = gain_total
    for copy in copies:
        copy.wait_send()


BLOCK = 128
SPAN = BLOCK + WINDOW
NN = (((1,), (0,)), ((), ()))
TN = (((0,), (0,)), ((), ()))


def mat(left, right, dims):
    return lax.dot_general(left, right, dims, preferred_element_type=F32)


def rope_tables(lengths, slots):
    slot_ids = jnp.arange(slots, dtype=jnp.int32)
    first_end, second_end = lengths[0, 0], lengths[0, 0] + lengths[0, 1]
    start = jnp.where(
        slot_ids < first_end, 0, jnp.where(slot_ids < second_end, first_end, second_end)
    )
    lane = jnp.arange(2 * HEAD_DIM, dtype=jnp.int32) % HEAD_DIM
    half = HEAD_DIM // 2
    inv_freq = ROPE_BASE ** (-((lane % half).astype(F32) * 2.0) / HEAD_DIM)
    angles = (slot_ids - start).astype(F32)[:, None] * inv_freq[None, :]
    return jnp.cos(angles), jnp.sin(angles) * jnp.where(lane < half, -1.0, 1.0)[None, :]


def swap_halves(values):
    half = HEAD_DIM // 2
    lane = lax.broadcasted_iota(jnp.int32, values.shape, 1)
    ahead = pltpu.roll(values, 2 * HEAD_DIM - half, 1)
    behind = pltpu.roll(values, half, 1)
    return jnp.where(lax.rem(lane, HEAD_DIM) < half, ahead, behind)


def allowed_pairs(lens, first, start):
    row = first + lax.broadcasted_iota(jnp.int32, (BLOCK, SPAN), 0)
    col = start + lax.broadcasted_iota(jnp.int32, (BLOCK, SPAN), 1)
    one, two = lens[0, 0], lens[0, 0] + lens[0, 1]
    ids = lambda v: (v >= one).astype(jnp.int32) + (v >= two).astype(jnp.int32)
    return (ids(row) == ids(col)) & (jnp.abs(row - col) <= WINDOW // 2)


def blocks_of(slots):
    for first in range(0, slots, BLOCK):
        yield first, min(max(first - WINDOW // 2, 0), slots - SPAN)


def softmax_block(q, k, allowed):
    scores = jnp.where(allowed, mat(q, k, NT) * HEAD_DIM ** (-0.5), MASKED)
    grown = jnp.exp(scores - jnp.max(scores, axis=-1, keepdims=True))
    return grown * (1.0 / jnp.sum(grown, axis=-1, keepdims=True))


def forward_kernel(nq, lens, xfull, w, cos, sin, qkv, att):
    slots = xfull.shape[0]
    proj = mat(xfull[...], w[:, : 3 * nq], NN)
    for at in range(0, 2 * nq, 128):
        piece = proj[:, at : at + 128]
        qkv[:, at : at + 128] = (piece * cos[...] + swap_halves(piece) * sin[...]).astype(BF)
    qkv[:, 2 * nq :] = proj[:, 2 * nq :].astype(BF)
    for first, start in blocks_of(slots):
        allowed = allowed_pairs(lens, first, start)
        for h in range(0, nq, HEAD_DIM):
            q = qkv[first : first + BLOCK, h : h + HEAD_DIM]
            k = qkv[start : start + SPAN, nq + h : nq + h + HEAD_DIM]
            v = qkv[start : start + SPAN, 2 * nq + h : 2 * nq + h + HEAD_DIM]
            probs = softmax_block(q, k, allowed).astype(BF)
            att[first : first + BLOCK, h : h + HEAD_DIM] = mat(probs, v, NN).astype(BF)


def backward_kernel(
    nq, lens, qkv, dbfull, att, w, cos, sin, xfull,
    dproj, grads, dqk, dv, datt,
):
    slots = xfull.shape[0]
    scale = HEAD_DIM ** (-0.5)
    datt[...] = mat(dbfull[...], w[:, 3 * nq : 4 * nq], NN).astype(BF)
    dqk[:, nq:] = jnp.zeros((slots, nq), F32)
    dv[...] = jnp.zeros((slots, nq), F32)
    for first, start in blocks_of(slots):
        allowed = allowed_pairs(lens, first, start)
        here, there = slice(first, first + BLOCK), slice(start, start + SPAN)
        for h in range(0, nq, HEAD_DIM):
            q = qkv[here, h : h + HEAD_DIM]
            k = qkv[there, nq + h : nq + h + HEAD_DIM]
            v = qkv[there, 2 * nq + h : 2 * nq + h + HEAD_DIM]
            g = datt[here, h : h + HEAD_DIM]
            p = softmax_block(q, k, allowed)
            dp = mat(g, v, NT)
            inner = jnp.sum(p * dp, axis=-1, keepdims=True)
            ds = (p * (dp - inner)).astype(BF)
            dqk[here, h : h + HEAD_DIM] = mat(ds, k, NN) * scale
            dqk[there, nq + h : nq + h + HEAD_DIM] += mat(ds, q, TN) * scale
            dv[there, h : h + HEAD_DIM] += mat(p.astype(BF), g, TN)
    for at in range(0, 2 * nq, 128):
        piece = dqk[:, at : at + 128]
        dproj[:, at : at + 128] = (piece * cos[...] - swap_halves(piece) * sin[...]).astype(BF)
    dproj[:, 2 * nq :] = dv[...].astype(BF)
    grads[:, : 3 * nq] = mat(xfull[...], dproj[...], TN).astype(BF)
    grads[:, 3 * nq :] = mat(dbfull[...], att[...], TN).astype(BF)


def gate_kernel(nf, x2full, cfull, w2, gated, dmix, grads):
    slots = x2full.shape[0]
    step = slots // 4
    for first in range(0, slots, step):
        here = slice(first, first + step)
        inputs = mat(x2full[here, :], w2[:, :nf], NN)
        gates = mat(x2full[here, :], w2[:, nf : 2 * nf], NN)
        d_gated = mat(cfull[here, :], w2[:, 2 * nf :], NN)
        below = 0.5 * (1.0 + lax.erf(inputs * 0.5**0.5))
        density = jnp.exp(-0.5 * inputs * inputs) * 0.3989422804014327
        gelu = inputs * below
        gated[here, :] = (gelu * gates).astype(BF)
        dmix[here, :nf] = ((below + inputs * density) * gates * d_gated).astype(BF)
        dmix[here, nf:] = (gelu * d_gated).astype(BF)
    grads[:, : 2 * nf] = mat(x2full[...], dmix[...], TN).astype(BF)
    grads[:, 2 * nf :] = mat(cfull[...], gated[...], TN).astype(BF)


def on_device(tokens, lengths, w_qkv, w_attn_out, w_in, w_mlp_out, gain_attn, gain_mlp, cotangent):
    dp_size, tensor_size = lax.axis_size("dp"), lax.axis_size("tensor")
    rows, width = tokens.shape
    own = w_qkv.shape[0]
    slots = rows * tensor_size
    nq, nf = w_qkv.shape[2], w_in.shape[2]
    c_attn, c_one, c_in, c_two = 3 * nq, 4 * nq, 2 * nf, 3 * nf
    gain_one = gain_attn.astype(F32)[:, None]
    gain_two = gain_mlp.astype(F32)[:, None]
    qkv_own = w_qkv.reshape(own, 3 * nq).astype(F32)
    in_own = w_in.reshape(own, 2 * nf).astype(F32)
    slab_one = jnp.concatenate([(qkv_own * gain_one).astype(BF), w_attn_out.T], axis=1)
    slab_two = jnp.concatenate([(in_own * gain_two).astype(BF), w_mlp_out.T], axis=1)
    full = jax.ShapeDtypeStruct((tensor_size, rows, width), BF)
    half = dp_size // 2
    xfull, cfull, wfull = pl.pallas_call(
        functools.partial(first_kernel, dp_size),
        out_shape=(full, full, jax.ShapeDtypeStruct((dp_size, own, c_one), BF)),
        in_specs=[VMEM, VMEM, ANY],
        out_specs=(ANY, ANY, ANY),
        scratch_shapes=[pltpu.VMEM((rows, width), BF)]
        + GATHER_SEMS * 2
        + dp_gather_sems(half),
        compiler_params=params(0),
    )(tokens, cotangent, slab_one)
    xfull = xfull.reshape(slots, width)
    cfull = cfull.reshape(slots, width)
    wfull = wfull.reshape(width, c_one)

    cos_tab, sin_tab = rope_tables(lengths, slots)
    big = pltpu.CompilerParams(vmem_limit_bytes=56 * 1024 * 1024)
    smem = pl.BlockSpec(memory_space=pltpu.SMEM)
    qkv, attended = pl.pallas_call(
        functools.partial(forward_kernel, nq),
        out_shape=(
            jax.ShapeDtypeStruct((slots, 3 * nq), BF),
            jax.ShapeDtypeStruct((slots, nq), BF),
        ),
        in_specs=[smem] + [VMEM] * 4,
        out_specs=(VMEM, VMEM),
        compiler_params=big,
    )(lengths, xfull, wfull, cos_tab, sin_tab)

    hid, x2full, w2full = pl.pallas_call(
        functools.partial(hidden_kernel, dp_size, c_attn, c_one),
        out_shape=(
            jax.ShapeDtypeStruct((rows, width), F32),
            full,
            jax.ShapeDtypeStruct((dp_size, own, c_two), BF),
        ),
        in_specs=[VMEM] * 3 + [ANY],
        out_specs=(VMEM, ANY, ANY),
        scratch_shapes=[pltpu.VMEM((rows, width), BF)]
        + GATHER_SEMS
        + scatter_scratch(rows, width)
        + dp_gather_sems(half),
        compiler_params=params(1),
    )(attended, wfull, tokens, slab_two)
    x2full = x2full.reshape(slots, width)
    w2full = w2full.reshape(width, c_two)

    gated, d_mixed, grads_two = pl.pallas_call(
        functools.partial(gate_kernel, nf),
        out_shape=(
            jax.ShapeDtypeStruct((slots, nf), BF),
            jax.ShapeDtypeStruct((slots, 2 * nf), BF),
            jax.ShapeDtypeStruct((width, c_two), BF),
        ),
        in_specs=[VMEM] * 3,
        out_specs=(VMEM,) * 3,
        compiler_params=big,
    )(x2full, cfull, w2full)

    dhid, dbfull, gsum_two = pl.pallas_call(
        functools.partial(middle_kernel, dp_size, c_in),
        out_shape=(
            jax.ShapeDtypeStruct((rows, width), F32),
            full,
            jax.ShapeDtypeStruct((own, c_two), F32),
        ),
        in_specs=[VMEM] * 5,
        out_specs=(VMEM, ANY, VMEM),
        scratch_shapes=[pltpu.VMEM((rows, width), BF)]
        + GATHER_SEMS
        + scatter_scratch(rows, width)
        + dp_scatter_scratch(half, own, c_two),
        compiler_params=params(2),
    )(d_mixed, w2full, hid, cotangent, grads_two.reshape(dp_size, own, c_two))
    dbfull = dbfull.reshape(slots, width)

    d_proj, grads_one = pl.pallas_call(
        functools.partial(backward_kernel, nq),
        out_shape=(
            jax.ShapeDtypeStruct((slots, 3 * nq), BF),
            jax.ShapeDtypeStruct((width, c_one), BF),
        ),
        in_specs=[smem] + [VMEM] * 7,
        out_specs=(VMEM, VMEM),
        scratch_shapes=[
            pltpu.VMEM((slots, 2 * nq), F32),
            pltpu.VMEM((slots, nq), F32),
            pltpu.VMEM((slots, nq), BF),
        ],
        compiler_params=big,
    )(lengths, qkv, dbfull, attended, wfull, cos_tab, sin_tab, xfull)

    others = tensor_size - 1
    grad_tokens, output, gsum_one, gains = pl.pallas_call(
        functools.partial(last_kernel, dp_size, tensor_size, c_attn, c_in),
        out_shape=(
            jax.ShapeDtypeStruct((rows, width), BF),
            jax.ShapeDtypeStruct((rows, width), BF),
            jax.ShapeDtypeStruct((own, c_one), F32),
            jax.ShapeDtypeStruct((own, 128), F32),
        ),
        in_specs=[VMEM] * 11,
        out_specs=(VMEM,) * 4,
        scratch_shapes=[
            pltpu.VMEM((own, 128), F32),
            pltpu.VMEM((others, own, 128), F32),
            pltpu.SemaphoreType.DMA((others,)),
            pltpu.SemaphoreType.DMA((others,)),
        ]
        + scatter_scratch(rows, width) * 2
        + dp_scatter_scratch(half, own, c_one),
        compiler_params=params(3),
    )(
        d_proj, wfull, tokens, dhid, grads_one.reshape(dp_size, own, c_one), gated, w2full, hid,
        qkv_own, in_own, gsum_two,
    )
    return (
        output,
        grad_tokens,
        (gsum_one[:, :c_attn] * gain_one).reshape(own, 3, nq),
        gsum_one[:, c_attn:].T,
        (gsum_two[:, :c_in] * gain_two).reshape(own, 2, nf),
        gsum_two[:, c_in:].T,
        gains[:, 0],
        gains[:, 64],
    )


def solution(mesh):
    return jax.shard_map(
        on_device,
        mesh=mesh,
        in_specs=(
            P(("dp", "tensor"), None),
            P("dp", None),
            P("dp", None, "tensor"),
            P("tensor", "dp"),
            P("dp", None, "tensor"),
            P("tensor", "dp"),
            P("dp"),
            P("dp"),
            P(("dp", "tensor"), None),
        ),
        out_specs=(
            P(("dp", "tensor"), None),
            P(("dp", "tensor"), None),
            P("dp", None, "tensor"),
            P("tensor", "dp"),
            P("dp", None, "tensor"),
            P("tensor", "dp"),
            P("dp"),
            P("dp"),
        ),
        check_vma=False,
    )
```

profile of v0, /device:TPU:8, one launch (start us, length us, event | category | flops | bytes accessed | tf_op | source)
XLA Modules:
  0.0 177.8 jit_solution(303288083262961825)
XLA Ops:
  0.6 0.7 convert_element_type.38
  1.3 0.7 convert_element_type.44
  2.0 1.3 fusion.7
  4.6 0.7 subtract_convert_fusion
  5.3 0.9 copy.25
  6.2 1.0 copy.26
  7.2 1.0 reshape.105.raw_two
  8.4 0.1 copy.23
  8.6 0.2 copy.24.raw_one
  8.9 3.1 %fusion = (f32[1024,128]{1,0:T(8,128)}, f32[1024,128]{1,0:T(8,128)}) fusion(f32[128]{0:T(128)S(1)} %get-tuple-element.70, f32[128]{0:T(128)S(1)} %get-tuple-element.71, f32[1024]{0:T(1024)S(1)} %subtract_convert_fusion), kind=kLoop, calls=%fused_computation.2 | loop fusion | flops 262144 | bytes 1053696 | tf_op jit(solution)/shard_map/mul | solution.py:360
  12.0 23.5 %shard_map.152 = (bf16[4,256,768]{2,1,0:T(8,128)(2,1)S(1)}, bf16[4,256,768]{2,1,0:T(8,128)(2,1)S(1)}, bf16[8,96,768]{2,1,0:T(8,128)(2,1)S(1)}) custom-call(bf16[256,768]{1,0:T(8,128)(2,1)S(1)} %copy-done.6, bf16[256,768]{1,0:T(8,128)(2,1)S(1)} %copy-done.8, bf16[96,768]{1,0:T(8,128)(2,1)S(1)} %pad_maximum_fusion.1.slab), custom_call_target="tpu_custom_call" | custom-call | tf_op jit(solution)/shard_map/pallas_call | solution.py:472
  35.5 1.0 copy-done
  36.5 1.2 copy-done.5
  37.7 1.1 copy-done.9
  38.8 10.5 %shard_map.153 = (bf16[1024,576]{1,0:T(8,128)(2,1)}, bf16[1024,192]{1,0:T(8,128)(2,1)}) custom-call(s32[1,2]{1,0:T(1,128)} %lens.3, bf16[1024,768]{1,0:T(8,128)(2,1)} %bitcast.25, bf16[768,768]{1,0:T(8,128)(2,1)} %bitcast.18, f32[1024,128]{1,0:T(8,128)} %get-tuple-element.67.cos, f32[1024,128]{1,0:T(8,128)} %get-tuple-element.66.sin), custom_call_target="tpu_custom_call" | custom-call | tf_op jit(solution)/shard_map/pallas_call | solution.py:489
  49.3 1.0 copy-done.7
  50.4 28.6 %shard_map.154 = (f32[256,768]{1,0:T(8,128)S(1)}, bf16[4,256,768]{2,1,0:T(8,128)(2,1)S(1)}, bf16[8,96,864]{2,1,0:T(8,128)(2,1)S(1)}) custom-call(bf16[1024,192]{1,0:T(8,128)(2,1)S(1)} %copy-done.7, bf16[768,768]{1,0:T(8,128)(2,1)S(1)} %bitcast.20, bf16[256,768]{1,0:T(8,128)(2,1)S(1)} %copy-done.6, bf16[96,864]{1,0:T(8,128)(2,1)S(1)} %pad_maximum_fusion.slab), custom_call_target="tpu_custom_call" | custom-call | tf_op jit(solution)/shard_map/pallas_call | solution.py:500
  79.0 1.1 copy-done.3
  80.1 1.2 copy-done.10
  81.2 8.5 %shard_map.155 = (bf16[1024,288]{1,0:T(8,128)(2,1)}, bf16[1024,576]{1,0:T(8,128)(2,1)}, bf16[768,864]{1,0:T(8,128)(2,1)}) custom-call(bf16[1024,768]{1,0:T(8,128)(2,1)} %bitcast.28, bf16[1024,768]{1,0:T(8,128)(2,1)} %bitcast.27, bf16[768,864]{1,0:T(8,128)(2,1)} %bitcast.22), custom_call_target="tpu_custom_call" | custom-call | tf_op jit(solution)/shard_map/pallas_call | solution.py:518
  89.7 1.3 copy-done.11
  91.0 30.1 %shard_map.156 = (f32[256,768]{1,0:T(8,128)S(1)}, bf16[4,256,768]{2,1,0:T(8,128)(2,1)}, f32[96,864]{1,0:T(8,128)S(1)}) custom-call(bf16[1024,576]{1,0:T(8,128)(2,1)S(1)} %copy-done.11, bf16[768,864]{1,0:T(8,128)(2,1)S(1)} %bitcast.24, f32[256,768]{1,0:T(8,128)S(1)} %get-tuple-element.36.hid, bf16[256,768]{1,0:T(8,128)(2,1)S(1)} %copy-done.8, ...), custom_call_target="tpu_custom_call" | custom-call | tf_op jit(solution)/shard_map/pallas_call | solution.py:530
  121.1 20.8 %shard_map.157 = (bf16[1024,576]{1,0:T(8,128)(2,1)}, bf16[768,768]{1,0:T(8,128)(2,1)}) custom-call(s32[1,2]{1,0:T(1,128)} %lens.3, bf16[1024,576]{1,0:T(8,128)(2,1)} %get-tuple-element.30.qkv, bf16[1024,768]{1,0:T(8,128)(2,1)} %bitcast.29, bf16[1024,192]{1,0:T(8,128)(2,1)} %get-tuple-element.31.att, bf16[768,768]{1,0:T(8,128)(2,1)} %bitcast.19, ...), custom_call_target="tpu_custom_call" | custom-call | tf_op jit(solution)/shard_map/pallas_call | solution.py:547
  141.9 29.8 %shard_map.158 = (bf16[256,768]{1,0:T(8,128)(2,1)S(1)}, bf16[256,768]{1,0:T(8,128)(2,1)S(1)}, f32[96,768]{1,0:T(8,128)S(1)}, f32[96,128]{1,0:T(8,128)S(1)}) custom-call(bf16[1024,576]{1,0:T(8,128)(2,1)} %get-tuple-element.39.dproj, bf16[768,768]{1,0:T(8,128)(2,1)S(1)} %bitcast.21, bf16[256,768]{1,0:T(8,128)(2,1)S(1)} %copy-done.6, ...), custom_call_target="tpu_custom_call" | custom-call | tf_op jit(solution)/shard_map/pallas_call | solution.py:564
  171.7 0.7 slice_reduce_fusion
  172.6 0.7 copy.30
  173.3 0.1 copy.28
  173.5 0.9 copy.29
  174.6 0.8 copy.31
  175.3 0.9 reshape.103
  176.3 0.7 copy.34
  177.0 0.7 copy.35
  (30 shorter events, 0.8 us)
Async XLA Ops:
  0.6 7.8 %copy-start.13 = (bf16[96,3,192]{2,0,1:T(8,128)(2,1)S(1)}, bf16[96,3,192]{2,0,1:T(8,128)(2,1)}, u32[]{:S(2)}) copy-start(bf16[96,3,192]{2,0,1:T(8,128)(2,1)} %param.11) | copy-start | bytes 331780
  8.4 3.6 %copy-start.6 = (bf16[256,768]{1,0:T(8,128)(2,1)S(1)}, bf16[256,768]{1,0:T(8,128)(2,1)}, u32[]{:S(2)}) copy-start(bf16[256,768]{1,0:T(8,128)(2,1)} %tok.5) | copy-start | bytes 1179652
  8.4 3.6 %copy-start.8 = (bf16[256,768]{1,0:T(8,128)(2,1)S(1)}, bf16[256,768]{1,0:T(8,128)(2,1)}, u32[]{:S(2)}) copy-start(bf16[256,768]{1,0:T(8,128)(2,1)} %cot.3) | copy-start | bytes 1179652
  35.5 1.0 copy-start
  36.5 1.2 copy-start.5
  37.7 1.1 copy-start.9
  38.8 10.5 %copy-start.1 = (bf16[8,96,768]{2,1,0:T(8,128)(2,1)S(1)}, bf16[8,96,768]{2,1,0:T(8,128)(2,1)}, u32[]{:S(2)}) copy-start(bf16[8,96,768]{2,1,0:T(8,128)(2,1)} %copy-done) | copy-start | bytes 3538948
  49.3 1.0 copy-start.7
  78.9 1.1 copy-start.3
  80.1 1.2 copy-start.10
  81.2 8.5 %copy-start.4 = (bf16[8,96,864]{2,1,0:T(8,128)(2,1)S(1)}, bf16[8,96,864]{2,1,0:T(8,128)(2,1)}, u32[]{:S(2)}) copy-start(bf16[8,96,864]{2,1,0:T(8,128)(2,1)} %copy-done.3) | copy-start | bytes 3981316
  89.7 1.3 copy-start.11
  121.1 20.8 %copy-start.2 = (bf16[8,96,768]{2,1,0:T(8,128)(2,1)S(1)}, bf16[8,96,768]{2,1,0:T(8,128)(2,1)}, u32[]{:S(2)}) copy-start(bf16[8,96,768]{2,1,0:T(8,128)(2,1)} %copy-done) | copy-start | bytes 3538948
  121.1 20.8 %copy-start.12 = (bf16[1024,288]{1,0:T(8,128)(2,1)S(1)}, bf16[1024,288]{1,0:T(8,128)(2,1)}, u32[]{:S(2)}) copy-start(bf16[1024,288]{1,0:T(8,128)(2,1)} %get-tuple-element.42.gated) | copy-start | bytes 1769476
where the time goes:
time: 180 us; the launch traced here: 178 us
  Pallas kernels  152 us (84%)
  local copies, waits for them, and re-layouts  18.3 us (10%)
  other arithmetic  5.63 us (3%)
  between operations  2.14 us (1%)
    pallas_call x1, Pallas kernels, on_device(): pl.pallas_call(functools.partial(middle_kernel, dp_size, c_in), out_shape...  30.1 us
    pallas_call x1, Pallas kernels, on_device(): pl.pallas_call(functools.partial(last_kernel, dp_size, tensor_size, c_att...  29.8 us
    pallas_call x1, Pallas kernels, on_device(): pl.pallas_call(functools.partial(hidden_kernel, dp_size, c_attn, c_one),...  28.6 us
    pallas_call x1, Pallas kernels, on_device(): pl.pallas_call(functools.partial(first_kernel, dp_size), out_shape=(full,...  23.5 us
    pallas_call x1, Pallas kernels, on_device(): pl.pallas_call(functools.partial(backward_kernel, nq), out_shape=(jax.Sha...  20.8 us
    unnamed x35, local copies, waits for them, and re-layouts  13.7 us
    pallas_call x1, Pallas kernels, on_device(): pl.pallas_call(functools.partial(forward_kernel, nq), out_shape=(jax.Shap...  10.5 us
    pallas_call x1, Pallas kernels, on_device(): pl.pallas_call(functools.partial(gate_kernel, nf), out_shape=(jax.ShapeDt...  8.5 us

commit v1 on v0

--- a/solution.py
+++ b/solution.py
@@ -73,34 +73,57 @@
     return [(hi * 2 + 1 - lo, t)] + [(lax.rem(hi + k, high) * 2 + lo, t) for k in range(1, high)]
 
 
+PIECES = 2
+
+
+def piece_rows(rows):
+    step = rows // PIECES
+    return [(c, pl.ds(c * step, step)) for c in range(PIECES)]
+
+
 class Gather:
     def __init__(self, src, out, sems):
         dp, t, x, core, corep, xp = tensor_place()
         send, recv, here = sems
         self.own = pltpu.make_async_copy(src, out.at[t], here)
-        self.over_x = remote(src, out.at[t], send.at[0], recv.at[0], (dp, xp))
-        self.to_core = remote(src, out.at[t], send.at[1], recv.at[1], (dp, corep))
-        self.relay = remote(out.at[xp], out.at[xp], send.at[2], recv.at[2], (dp, corep))
+        last = 2 * PIECES
+        self.to_core = remote(src, out.at[t], send.at[last], recv.at[last], (dp, corep))
+        self.over_x, self.relay = [], []
+        for c, cut in piece_rows(src.shape[0]):
+            self.over_x.append(
+                remote(src.at[cut], out.at[t, cut], send.at[c], recv.at[c], (dp, xp))
+            )
+            at = PIECES + c
+            self.relay.append(
+                remote(out.at[xp, cut], out.at[xp, cut], send.at[at], recv.at[at], (dp, corep))
+            )
 
     def start(self):
-        self.over_x.start()
+        for copy in self.over_x:
+            copy.start()
         self.to_core.start()
         self.own.start()
 
     def forward(self):
-        self.over_x.wait_recv()
-        self.relay.start()
+        for arrived, copy in zip(self.over_x, self.relay):
+            arrived.wait_recv()
+            copy.start()
 
     def finish(self):
         self.to_core.wait_recv()
-        self.relay.wait_recv()
-        self.over_x.wait_send()
-        self.to_core.wait_send()
-        self.relay.wait_send()
+        for copy in self.relay:
+            copy.wait_recv()
+        for copy in self.over_x + self.relay + [self.to_core]:
+            copy.wait_send()
         self.own.wait()
 
 
-GATHER_SEMS = [pltpu.SemaphoreType.DMA((3,)), pltpu.SemaphoreType.DMA((3,)), pltpu.SemaphoreType.DMA]
+TENSOR_COPIES = 2 * PIECES + 1
+GATHER_SEMS = [
+    pltpu.SemaphoreType.DMA((TENSOR_COPIES,)),
+    pltpu.SemaphoreType.DMA((TENSOR_COPIES,)),
+    pltpu.SemaphoreType.DMA,
+]
 
 
 class ScatterSum:
@@ -110,28 +133,43 @@
         dp, t, x, core, corep, xp = tensor_place()
         self.place = (t, x, core, corep, xp)
         pair = (dp, corep)
-        self.far = remote(self.sbuf.at[0], self.r1.at[0], send.at[0], recv.at[0], pair)
-        self.near = remote(self.sbuf.at[1], self.r1.at[1], send.at[1], recv.at[1], pair)
-        self.over = remote(self.pbuf, self.r2, send.at[2], recv.at[2], (dp, xp))
+        last = 2 * PIECES
+        self.near = remote(self.sbuf.at[1], self.r1.at[1], send.at[last], recv.at[last], pair)
+        self.far, self.over = [], []
+        self.rows = self.pbuf.shape[0]
+        for c, cut in piece_rows(self.rows):
+            self.far.append(
+                remote(self.sbuf.at[0, cut], self.r1.at[0, cut], send.at[c], recv.at[c], pair)
+            )
+            at = PIECES + c
+            self.over.append(
+                remote(self.pbuf.at[cut], self.r2.at[cut], send.at[at], recv.at[at], (dp, xp))
+            )
 
     def begin(self):
         t, x, core, corep, xp = self.place
-        self.sbuf[0] = self.part((1 - x) * 2 + 1 - core).astype(BF)
-        self.far.start()
-        mine = self.part(xp)
-        self.far.wait_recv()
-        self.pbuf[...] = (mine + self.r1[0].astype(F32)).astype(BF)
-        self.over.start()
-        self.sbuf[1] = self.part(corep).astype(BF)
+        step = self.rows // PIECES
+        for c in range(PIECES):
+            low, high = c * step, (c + 1) * step
+            self.sbuf[0, low:high] = self.part((1 - x) * 2 + 1 - core, low, step).astype(BF)
+            self.far[c].start()
+        for c in range(PIECES):
+            low, high = c * step, (c + 1) * step
+            mine = self.part(xp, low, step)
+            self.far[c].wait_recv()
+            self.pbuf[low:high] = (mine + self.r1[0, low:high].astype(F32)).astype(BF)
+            self.over[c].start()
+        self.sbuf[1] = self.part(corep, 0, self.rows).astype(BF)
         self.near.start()
 
     def finish(self):
-        total = self.part(self.place[0])
+        total = self.part(self.place[0], 0, self.rows)
         self.near.wait_recv()
         total = total + self.r1[1].astype(F32)
-        self.over.wait_recv()
+        for copy in self.over:
+            copy.wait_recv()
         total = total + self.r2[...].astype(F32)
-        for copy in (self.far, self.near, self.over):
+        for copy in self.far + self.over + [self.near]:
             copy.wait_send()
         return total
 
@@ -229,8 +267,8 @@
         pltpu.VMEM((2, rows, width), BF),
         pltpu.VMEM((rows, width), BF),
         pltpu.VMEM((rows, width), BF),
-        pltpu.SemaphoreType.DMA((3,)),
-        pltpu.SemaphoreType.DMA((3,)),
+        pltpu.SemaphoreType.DMA((TENSOR_COPIES,)),
+        pltpu.SemaphoreType.DMA((TENSOR_COPIES,)),
     ]
 
 
@@ -241,8 +279,8 @@
 
 
 def block_product(lhs_ref, w, low, high, rows):
-    def part(b):
-        lhs = lhs_ref[pl.ds(pl.multiple_of(b * rows, rows), rows), :]
+    def part(b, first, count):
+        lhs = lhs_ref[pl.ds(pl.multiple_of(b * rows + first, 128), count), :]
         return lax.dot_general(lhs, w[:, low:high], NT, preferred_element_type=F32)
 
     return part
@@ -353,11 +391,18 @@
     start = jnp.where(
         slot_ids < first_end, 0, jnp.where(slot_ids < second_end, first_end, second_end)
     )
-    lane = jnp.arange(2 * HEAD_DIM, dtype=jnp.int32) % HEAD_DIM
     half = HEAD_DIM // 2
-    inv_freq = ROPE_BASE ** (-((lane % half).astype(F32) * 2.0) / HEAD_DIM)
-    angles = (slot_ids - start).astype(F32)[:, None] * inv_freq[None, :]
-    return jnp.cos(angles), jnp.sin(angles) * jnp.where(lane < half, -1.0, 1.0)[None, :]
+    inv_freq = ROPE_BASE ** (-(jnp.arange(half, dtype=F32) * 2.0) / HEAD_DIM)
+    angles = inv_freq[:, None] * (slot_ids - start).astype(F32)[None, :]
+    return jnp.cos(angles), jnp.sin(angles)
+
+
+def two_heads(cos, sin):
+    cos_part, sin_part = cos[...], sin[...]
+    return (
+        jnp.concatenate([cos_part] * 4, axis=0).T,
+        jnp.concatenate([-sin_part, sin_part] * 2, axis=0).T,
+    )
 
 
 def swap_halves(values):
@@ -389,10 +434,11 @@
 
 def forward_kernel(nq, lens, xfull, w, cos, sin, qkv, att):
     slots = xfull.shape[0]
+    cos_tab, sin_tab = two_heads(cos, sin)
     proj = mat(xfull[...], w[:, : 3 * nq], NN)
     for at in range(0, 2 * nq, 128):
         piece = proj[:, at : at + 128]
-        qkv[:, at : at + 128] = (piece * cos[...] + swap_halves(piece) * sin[...]).astype(BF)
+        qkv[:, at : at + 128] = (piece * cos_tab + swap_halves(piece) * sin_tab).astype(BF)
     qkv[:, 2 * nq :] = proj[:, 2 * nq :].astype(BF)
     for first, start in blocks_of(slots):
         allowed = allowed_pairs(lens, first, start)
@@ -428,9 +474,10 @@
             dqk[here, h : h + HEAD_DIM] = mat(ds, k, NN) * scale
             dqk[there, nq + h : nq + h + HEAD_DIM] += mat(ds, q, TN) * scale
             dv[there, h : h + HEAD_DIM] += mat(p.astype(BF), g, TN)
+    cos_tab, sin_tab = two_heads(cos, sin)
     for at in range(0, 2 * nq, 128):
         piece = dqk[:, at : at + 128]
-        dproj[:, at : at + 128] = (piece * cos[...] - swap_halves(piece) * sin[...]).astype(BF)
+        dproj[:, at : at + 128] = (piece * cos_tab - swap_halves(piece) * sin_tab).astype(BF)
     dproj[:, 2 * nq :] = dv[...].astype(BF)
     grads[:, : 3 * nq] = mat(xfull[...], dproj[...], TN).astype(BF)
     grads[:, 3 * nq :] = mat(dbfull[...], att[...], TN).astype(BF)

time: 180 us -> 179 us (level)
  other arithmetic: 5.63 us -> 3.78 us
    mul x1 -> x0, other arithmetic: 3.09 us -> none  [rope_tables(): jnp.sin(angles) * jnp.where(lane < half, -1.0, 1.0)[None, :]]
where the time goes in v1:
time: 179 us; the launch traced here: 176 us
  Pallas kernels  151 us (84%)
  local copies, waits for them, and re-layouts  18.3 us (10%)
  other arithmetic  3.78 us (2%)
  between operations  2.14 us (1%)
    pallas_call x1, Pallas kernels, on_device(): pl.pallas_call(functools.partial(last_kernel, dp_size, tensor_size, c_att...  30.5 us
    pallas_call x1, Pallas kernels, on_device(): pl.pallas_call(functools.partial(hidden_kernel, dp_size, c_attn, c_one),...  29.5 us
    pallas_call x1, Pallas kernels, on_device(): pl.pallas_call(functools.partial(middle_kernel, dp_size, c_in), out_shape...  28.6 us
    pallas_call x1, Pallas kernels, on_device(): pl.pallas_call(functools.partial(first_kernel, dp_size), out_shape=(full,...  23.3 us
    pallas_call x1, Pallas kernels, on_device(): pl.pallas_call(functools.partial(backward_kernel, nq), out_shape=(jax.Sha...  20 us
    unnamed x35, local copies, waits for them, and re-layouts  13.7 us
    pallas_call x1, Pallas kernels, on_device(): pl.pallas_call(functools.partial(forward_kernel, nq), out_shape=(jax.Shap...  11 us
    pallas_call x1, Pallas kernels, on_device(): pl.pallas_call(functools.partial(gate_kernel, nf), out_shape=(jax.ShapeDt...  8.48 us

profile of v1, /device:TPU:8, one launch (start us, length us, event | category | flops | bytes accessed | tf_op | source)
XLA Modules:
  0.0 175.7 jit_solution(16724291990281743875)
XLA Ops:
  0.6 0.7 convert_element_type.31
  1.3 0.7 convert_element_type.36
  2.0 1.3 fusion
  4.6 0.7 subtract_convert_fusion
  5.3 0.9 copy.25
  6.2 1.0 copy.26
  7.2 1.0 reshape.83.raw_two
  8.4 1.2 multiply_sine_fusion
  9.7 0.1 copy.23
  9.8 0.2 copy.24.raw_one
  10.2 23.3 %shard_map.152 = (bf16[4,256,768]{2,1,0:T(8,128)(2,1)S(1)}, bf16[4,256,768]{2,1,0:T(8,128)(2,1)S(1)}, bf16[8,96,768]{2,1,0:T(8,128)(2,1)S(1)}) custom-call(bf16[256,768]{1,0:T(8,128)(2,1)S(1)} %copy-done.6, bf16[256,768]{1,0:T(8,128)(2,1)S(1)} %copy-done.8, bf16[96,768]{1,0:T(8,128)(2,1)S(1)} %pad_maximum_fusion.1.slab), custom_call_target="tpu_custom_call" | custom-call | tf_op jit(solution)/shard_map/pallas_call | solution.py:519
  33.4 1.0 copy-done
  34.5 1.2 copy-done.5
  35.6 1.1 copy-done.9
  36.8 11.0 %shard_map.153 = (bf16[1024,576]{1,0:T(8,128)(2,1)}, bf16[1024,192]{1,0:T(8,128)(2,1)}) custom-call(s32[1,2]{1,0:T(1,128)} %lens.3, bf16[1024,768]{1,0:T(8,128)(2,1)} %bitcast.25, bf16[768,768]{1,0:T(8,128)(2,1)} %bitcast.18, f32[32,1024]{1,0:T(8,128)} %get-tuple-element.67.cos, f32[32,1024]{1,0:T(8,128)} %get-tuple-element.66.sin), custom_call_target="tpu_custom_call" | custom-call | tf_op jit(solution)/shard_map/pallas_call | solution.py:536
  47.8 1.0 copy-done.7
  48.8 29.5 %shard_map.154 = (f32[256,768]{1,0:T(8,128)S(1)}, bf16[4,256,768]{2,1,0:T(8,128)(2,1)S(1)}, bf16[8,96,864]{2,1,0:T(8,128)(2,1)S(1)}) custom-call(bf16[1024,192]{1,0:T(8,128)(2,1)S(1)} %copy-done.7, bf16[768,768]{1,0:T(8,128)(2,1)S(1)} %bitcast.20, bf16[256,768]{1,0:T(8,128)(2,1)S(1)} %copy-done.6, bf16[96,864]{1,0:T(8,128)(2,1)S(1)} %pad_maximum_fusion.slab), custom_call_target="tpu_custom_call" | custom-call | tf_op jit(solution)/shard_map/pallas_call | solution.py:547
  78.3 1.1 copy-done.3
  79.4 1.2 copy-done.10
  80.6 8.5 %shard_map.155 = (bf16[1024,288]{1,0:T(8,128)(2,1)}, bf16[1024,576]{1,0:T(8,128)(2,1)}, bf16[768,864]{1,0:T(8,128)(2,1)}) custom-call(bf16[1024,768]{1,0:T(8,128)(2,1)} %bitcast.28, bf16[1024,768]{1,0:T(8,128)(2,1)} %bitcast.27, bf16[768,864]{1,0:T(8,128)(2,1)} %bitcast.22), custom_call_target="tpu_custom_call" | custom-call | tf_op jit(solution)/shard_map/pallas_call | solution.py:565
  89.0 1.3 copy-done.11
  90.4 28.6 %shard_map.156 = (f32[256,768]{1,0:T(8,128)S(1)}, bf16[4,256,768]{2,1,0:T(8,128)(2,1)}, f32[96,864]{1,0:T(8,128)S(1)}) custom-call(bf16[1024,576]{1,0:T(8,128)(2,1)S(1)} %copy-done.11, bf16[768,864]{1,0:T(8,128)(2,1)S(1)} %bitcast.24, f32[256,768]{1,0:T(8,128)S(1)} %get-tuple-element.36.hid, bf16[256,768]{1,0:T(8,128)(2,1)S(1)} %copy-done.8, ...), custom_call_target="tpu_custom_call" | custom-call | tf_op jit(solution)/shard_map/pallas_call | solution.py:577
  119.0 20.0 %shard_map.157 = (bf16[1024,576]{1,0:T(8,128)(2,1)}, bf16[768,768]{1,0:T(8,128)(2,1)}) custom-call(s32[1,2]{1,0:T(1,128)} %lens.3, bf16[1024,576]{1,0:T(8,128)(2,1)} %get-tuple-element.30.qkv, bf16[1024,768]{1,0:T(8,128)(2,1)} %bitcast.29, bf16[1024,192]{1,0:T(8,128)(2,1)} %get-tuple-element.31.att, bf16[768,768]{1,0:T(8,128)(2,1)} %bitcast.19, ...), custom_call_target="tpu_custom_call" | custom-call | tf_op jit(solution)/shard_map/pallas_call | solution.py:594
  139.1 30.5 %shard_map.158 = (bf16[256,768]{1,0:T(8,128)(2,1)S(1)}, bf16[256,768]{1,0:T(8,128)(2,1)S(1)}, f32[96,768]{1,0:T(8,128)S(1)}, f32[96,128]{1,0:T(8,128)S(1)}) custom-call(bf16[1024,576]{1,0:T(8,128)(2,1)} %get-tuple-element.39.dproj, bf16[768,768]{1,0:T(8,128)(2,1)S(1)} %bitcast.21, bf16[256,768]{1,0:T(8,128)(2,1)S(1)} %copy-done.6, ...), custom_call_target="tpu_custom_call" | custom-call | tf_op jit(solution)/shard_map/pallas_call | solution.py:611
  169.6 0.7 slice_reduce_fusion
  170.5 0.7 copy.30
  171.2 0.1 copy.28
  171.4 0.9 copy.29
  172.4 0.8 copy.31
  173.2 0.9 reshape.81
  174.2 0.7 copy.34
  174.9 0.7 copy.35
  (30 shorter events, 0.8 us)
Async XLA Ops:
  0.6 9.0 %copy-start.13 = (bf16[96,3,192]{2,0,1:T(8,128)(2,1)S(1)}, bf16[96,3,192]{2,0,1:T(8,128)(2,1)}, u32[]{:S(2)}) copy-start(bf16[96,3,192]{2,0,1:T(8,128)(2,1)} %param.11) | copy-start | bytes 331780
  8.2 1.9 %copy-start.6 = (bf16[256,768]{1,0:T(8,128)(2,1)S(1)}, bf16[256,768]{1,0:T(8,128)(2,1)}, u32[]{:S(2)}) copy-start(bf16[256,768]{1,0:T(8,128)(2,1)} %tok.5) | copy-start | bytes 1179652
  8.2 1.9 %copy-start.8 = (bf16[256,768]{1,0:T(8,128)(2,1)S(1)}, bf16[256,768]{1,0:T(8,128)(2,1)}, u32[]{:S(2)}) copy-start(bf16[256,768]{1,0:T(8,128)(2,1)} %cot.3) | copy-start | bytes 1179652
  33.4 1.0 copy-start
  34.5 1.2 copy-start.5
  35.6 1.1 copy-start.9
  36.8 11.0 %copy-start.1 = (bf16[8,96,768]{2,1,0:T(8,128)(2,1)S(1)}, bf16[8,96,768]{2,1,0:T(8,128)(2,1)}, u32[]{:S(2)}) copy-start(bf16[8,96,768]{2,1,0:T(8,128)(2,1)} %copy-done) | copy-start | bytes 3538948
  47.8 1.0 copy-start.7
  78.3 1.1 copy-start.3
  79.4 1.2 copy-start.10
  80.6 8.5 %copy-start.4 = (bf16[8,96,864]{2,1,0:T(8,128)(2,1)S(1)}, bf16[8,96,864]{2,1,0:T(8,128)(2,1)}, u32[]{:S(2)}) copy-start(bf16[8,96,864]{2,1,0:T(8,128)(2,1)} %copy-done.3) | copy-start | bytes 3981316
  89.0 1.3 copy-start.11
  119.0 20.1 %copy-start.2 = (bf16[8,96,768]{2,1,0:T(8,128)(2,1)S(1)}, bf16[8,96,768]{2,1,0:T(8,128)(2,1)}, u32[]{:S(2)}) copy-start(bf16[8,96,768]{2,1,0:T(8,128)(2,1)} %copy-done) | copy-start | bytes 3538948
  119.0 20.1 %copy-start.12 = (bf16[1024,288]{1,0:T(8,128)(2,1)S(1)}, bf16[1024,288]{1,0:T(8,128)(2,1)}, u32[]{:S(2)}) copy-start(bf16[1024,288]{1,0:T(8,128)(2,1)} %get-tuple-element.42.gated) | copy-start | bytes 1769476
